TPU v7x, 32 devices: a whole 2x2x4 slice. The times are simulated.
32 devices in a mesh: win: 1, col: 32 (over z, y, x, core).
Axes of the slice: x: 2, y: 2, z: 4, core: 2. Of those that a mesh axis runs over, the one named last changes fastest.
Arguments:
- records: bfloat16 [1024, 2048], P('win', 'col'), may hold values from -6 to 6
- quality_mask: int32 [1024], P('win'), may hold values 0 or 1
- band_start: int32 [1], P('win'), may hold values from 0 to 512
Outputs:
- correlations: bfloat16 [512, 1024, 256], P('win', 'col')
Inputs may be any that keep to these rules, and one draw needn't show every extreme that they name: `band_start`: the band lies inside the array.
All inputs are finite; a program needn't handle non-finite values.
Results may differ from a plain program's by a relative error of at most 0.0074.
Values may be sent and summed in bfloat16 or wider, within the bound.
A program may use at most 64 MiB of HBM per device.

v0:
```python
import math

import jax
import jax.numpy as jnp
from jax import lax
from jax.sharding import PartitionSpec as P

L = 1024
LAGS = 256
SEG = 2
ROWS = 512
F = 512


def dft_tables():
    sample_ids = jnp.arange(L, dtype=jnp.int32)
    bin_ids = jnp.arange(F, dtype=jnp.int32)
    phase = jnp.mod(sample_ids[:, None] * bin_ids[None, :], L).astype(jnp.float32) * (
        2.0 * jnp.pi / L
    )
    forward = jnp.concatenate([jnp.cos(phase), -jnp.sin(phase)], axis=1).astype(jnp.bfloat16)
    shifts = jnp.arange(LAGS, dtype=jnp.int32) - LAGS // 2
    turns = jnp.mod(bin_ids[:, None] * shifts[None, :], L).astype(jnp.float32) * (2.0 * jnp.pi / L)
    factor = 1.0 / jnp.sqrt(jnp.float32(SEG * F))
    inverse = (jnp.concatenate([jnp.cos(turns), -jnp.sin(turns)], axis=0) * factor).astype(
        jnp.bfloat16
    )
    return (forward, inverse)


def whitened_spectra(samples, forward):
    channels_here = samples.shape[0]
    spectra = jnp.dot(
        samples.reshape(channels_here * SEG, L), forward, preferred_element_type=jnp.float32
    )
    spectra = spectra.reshape(channels_here, SEG, 2 * F)
    real_part = spectra[:, :, :F]
    imag_part = spectra[:, :, F:]
    power_mean = jnp.mean(real_part * real_part + imag_part * imag_part, axis=1)
    level_mean = jnp.mean(power_mean, axis=1, keepdims=True)
    scaling = jnp.sqrt(power_mean + level_mean + 1e-06)
    return spectra / jnp.concatenate([scaling, scaling], axis=1)[:, None, :]


def correlate_block(band_block, col_values, inverse):
    row_values = band_block.astype(jnp.float32)
    row_real = row_values[:, None, :, :F]
    row_imag = row_values[:, None, :, F:]
    col_real = col_values[None, :, :, :F]
    col_imag = col_values[None, :, :, F:]
    cross_real = jnp.sum(row_real * col_real + row_imag * col_imag, axis=2)
    cross_imag = jnp.sum(row_imag * col_real - row_real * col_imag, axis=2)
    cross = jnp.concatenate([cross_real, cross_imag], axis=2).astype(jnp.bfloat16)
    rows_here = cross.shape[0]
    cols_here = cross.shape[1]
    result = jnp.dot(
        cross.reshape(rows_here * cols_here, 2 * F), inverse, preferred_element_type=jnp.float32
    )
    return result.reshape(rows_here, cols_here, LAGS).astype(jnp.bfloat16)


def on_device(records, quality_mask, band_start):
    devices_col = lax.axis_size("col")
    position = lax.axis_index("col")
    total_channels = records.shape[0]
    block_channels = total_channels // devices_col
    forward, inverse = dft_tables()
    block_start = position * block_channels
    block_keep = lax.dynamic_slice_in_dim(quality_mask, block_start, block_channels, 0).astype(
        jnp.float32
    )
    channel_records = lax.all_to_all(records, "col", split_axis=0, concat_axis=1, tiled=True)
    white_raw = whitened_spectra(channel_records, forward)
    white = (white_raw * block_keep[:, None, None]).astype(jnp.bfloat16)
    first_row = band_start[0]
    offsets = first_row + jnp.arange(ROWS, dtype=jnp.int32) - block_start
    inside = ((offsets >= 0) & (offsets < block_channels)).astype(jnp.float32)
    picked = jnp.take(white, jnp.clip(offsets, 0, block_channels - 1), axis=0).astype(jnp.float32)
    picked = picked * inside[:, None, None]
    band = lax.psum(picked, "col").astype(jnp.bfloat16)
    col_values = white.astype(jnp.float32)
    row_block = math.gcd(ROWS, 64)
    band_blocks = band.reshape(ROWS // row_block, row_block, SEG, 2 * F)
    results = lax.map(
        lambda band_block: correlate_block(band_block, col_values, inverse), band_blocks
    )
    return results.reshape(ROWS, block_channels, LAGS)


def solution(mesh):
    return jax.shard_map(
        on_device,
        mesh=mesh,
        in_specs=(P("win", "col"), P("win"), P("win")),
        out_specs=P("win", "col", None),
        check_vma=False,
    )
```

profile of v0, /device:TPU:1, one launch (start us, length us, event | category | flops | bytes accessed | tf_op | source)
XLA Modules:
  0.0 199.5 jit_solution(16109151196732330955)
XLA Ops:
  0.0 1.1 copy.9
  1.9 7.1 %all-to-all-start = ((bf16[32,2,1024]{2,1,0:T(2,128)(2,1)}), bf16[32,2,1024]{2,1,0:T(2,128)(2,1)S(1)}, u32[]{:S(2)}, u32[]{:S(2)}) async-start(bf16[32,2,1024]{2,1,0:T(2,128)(2,1)} %reshape.91), calls=%async_computation | async-start | bytes 262144 | tf_op jit(solution)/shard_map/all_to_all | solution.py:72
  9.7 2.1 %fusion.35 = (f32[512,256]{1,0:T(8,128)S(1)}, f32[512,256]{1,0:T(8,128)S(1)}) fusion(s32[256]{0:T(256)S(1)} %iota_add_fusion), kind=kLoop, calls=%fused_computation.43 | loop fusion | flops 1966080 | bytes 1049600 | tf_op jit(solution)/shard_map/cos | solution.py:25
  12.7 8.5 %negate_convert_fusion = (bf16[1024,512]{1,0:T(8,128)(2,1)S(1)}, bf16[1024,512]{1,0:T(8,128)(2,1)S(1)}) fusion(), kind=kLoop, calls=%fused_computation.25 | loop fusion | flops 8912896 | bytes 2097152 | tf_op jit(solution)/shard_map/convert.4
  23.1 16.3 %gather_fusion = bf16[512,2,1024]{2,1,0:T(2,128)(2,1)S(1)} fusion(bf16[32,2,1024]{2,1,0:T(2,128)(2,1)S(1)} %multiply_convert_fusion, s32[1024]{0:T(1024)S(1)} %pad_clamp_fusion), kind=kCustom, calls=%fused_computation | custom fusion | bytes 4196352 | tf_op jit(solution)/shard_map/jit(_take)/gather | solution.py:78
  39.4 4.3 %convert_multiply_fusion = f32[512,2,1024]{2,1,0:T(2,128)} fusion(f32[512]{0:T(512)S(1)} %get-tuple-element.56, bf16[512,2,1024]{2,1,0:T(2,128)(2,1)S(1)} %gather_fusion, pred[512]{0:T(512)(128)(4,1)S(1)} %get-tuple-element.57), kind=kLoop, calls=%fused_computation.13 | loop fusion | flops 3145728 | bytes 6294016 | tf_op jit(solution)/shard_map/mul | solution.py:79
  43.8 92.4 %all-reduce.1 = bf16[512,2,1024]{2,1,0:T(2,128)(2,1)S(1)} all-reduce(f32[512,2,1024]{2,1,0:T(2,128)} %convert_multiply_fusion), channel_id=1, replica_groups=mesh['win'=1,'col'=32] {'col'}, use_global_device_ids=true, to_apply=%region_2.3 | all-reduce | flops 1048576 | bytes 6291456 | tf_op jit(solution)/shard_map/psum | solution.py:80
  136.1 63.4 %while.10 = (s32[]{:T(128)}, bf16[8,64,32,256]{3,2,1,0:T(8,128)(2,1)}, bf16[8,64,2,1024]{3,2,1,0:T(2,128)(2,1)S(1)}, f32[32,2,1024]{2,0,1:T(8,128)S(1)}, bf16[1024,256]{1,0:T(8,128)(2,1)S(1)}, /*index=5*/s32[]{:T(128)}) while((s32[]{:T(128)}, bf16[8,64,32,256]{3,2,1,0:T(8,128)(2,1)}, bf16[8,64,2,1024]{3,2,1,0:T(2,128)(2,1)S(1)}, ...), condition=%wide.region_6.7_spmd, body=%wide.region_3.6_spmd.sunk | while | flops 1097465856 | bytes 13107785 | solution.py:84
  136.4 5.4 %add_reduce_fusion.2 = (bf16[64,32,512]{2,1,0:T(8,128)(2,1)S(1)}, bf16[64,32,512]{2,1,0:T(8,128)(2,1)S(1)}) fusion(f32[32,2,512]{2,0,1:T(8,128)S(1)} %get-tuple-element.97, f32[64,2,512]{2,1,0:T(2,128)S(1)} %get-tuple-element.98, f32[32,2,512]{2,0,1:T(8,128)S(1)} %get-tuple-element.99, f32[64,2,512]{2,1,0:T(2,128)S(1)} %get-tuple-element.100), kind=kLoop, calls=%fused_computation.2.clone.1 | loop fusion | flops 14680064 | bytes 4980736 | tf_op jit(solution)/shard_map/while/body/eval_jaxpr/reduce_sum | solution.py:51
  141.9 2.2 %fusion.55 = bf16[8,64,32,256]{3,2,1,0:T(8,128)(2,1)} fusion(bf16[8,64,32,256]{3,2,1,0:T(8,128)(2,1)} %get-tuple-element.110, s32[]{:T(128)} %get-tuple-element.109, bf16[64,32,512]{2,1,0:T(8,128)(2,1)S(1)} %get-tuple-element.101, bf16[64,32,512]{2,1,0:T(8,128)(2,1)S(1)} %get-tuple-element.102, bf16[1024,256]{1,0:T(8,128)(2,1)S(1)} %get-tuple-element.119), kind=kOutput, calls=%fused_computation.9.clone.1 | convolution fusion | flops 1082654720 | bytes 5767680 | tf_op jit(solution)/shard_map/while/body/eval_jaxpr/dot_general | solution.py:56
  144.3 5.4 %add_reduce_fusion.2 = (bf16[64,32,512]{2,1,0:T(8,128)(2,1)S(1)}, bf16[64,32,512]{2,1,0:T(8,128)(2,1)S(1)}) fusion(f32[32,2,512]{2,0,1:T(8,128)S(1)} %get-tuple-element.97, f32[64,2,512]{2,1,0:T(2,128)S(1)} %get-tuple-element.98, f32[32,2,512]{2,0,1:T(8,128)S(1)} %get-tuple-element.99, f32[64,2,512]{2,1,0:T(2,128)S(1)} %get-tuple-element.100), kind=kLoop, calls=%fused_computation.2.clone.1 | loop fusion | flops 14680064 | bytes 4980736 | tf_op jit(solution)/shard_map/while/body/eval_jaxpr/reduce_sum | solution.py:51
  149.8 2.2 %fusion.55 = bf16[8,64,32,256]{3,2,1,0:T(8,128)(2,1)} fusion(bf16[8,64,32,256]{3,2,1,0:T(8,128)(2,1)} %get-tuple-element.110, s32[]{:T(128)} %get-tuple-element.109, bf16[64,32,512]{2,1,0:T(8,128)(2,1)S(1)} %get-tuple-element.101, bf16[64,32,512]{2,1,0:T(8,128)(2,1)S(1)} %get-tuple-element.102, bf16[1024,256]{1,0:T(8,128)(2,1)S(1)} %get-tuple-element.119), kind=kOutput, calls=%fused_computation.9.clone.1 | convolution fusion | flops 1082654720 | bytes 5767680 | tf_op jit(solution)/shard_map/while/body/eval_jaxpr/dot_general | solution.py:56
  152.3 5.4 %add_reduce_fusion.2 = (bf16[64,32,512]{2,1,0:T(8,128)(2,1)S(1)}, bf16[64,32,512]{2,1,0:T(8,128)(2,1)S(1)}) fusion(f32[32,2,512]{2,0,1:T(8,128)S(1)} %get-tuple-element.97, f32[64,2,512]{2,1,0:T(2,128)S(1)} %get-tuple-element.98, f32[32,2,512]{2,0,1:T(8,128)S(1)} %get-tuple-element.99, f32[64,2,512]{2,1,0:T(2,128)S(1)} %get-tuple-element.100), kind=kLoop, calls=%fused_computation.2.clone.1 | loop fusion | flops 14680064 | bytes 4980736 | tf_op jit(solution)/shard_map/while/body/eval_jaxpr/reduce_sum | solution.py:51
  157.7 2.2 %fusion.55 = bf16[8,64,32,256]{3,2,1,0:T(8,128)(2,1)} fusion(bf16[8,64,32,256]{3,2,1,0:T(8,128)(2,1)} %get-tuple-element.110, s32[]{:T(128)} %get-tuple-element.109, bf16[64,32,512]{2,1,0:T(8,128)(2,1)S(1)} %get-tuple-element.101, bf16[64,32,512]{2,1,0:T(8,128)(2,1)S(1)} %get-tuple-element.102, bf16[1024,256]{1,0:T(8,128)(2,1)S(1)} %get-tuple-element.119), kind=kOutput, calls=%fused_computation.9.clone.1 | convolution fusion | flops 1082654720 | bytes 5767680 | tf_op jit(solution)/shard_map/while/body/eval_jaxpr/dot_general | solution.py:56
  160.2 5.4 %add_reduce_fusion.2 = (bf16[64,32,512]{2,1,0:T(8,128)(2,1)S(1)}, bf16[64,32,512]{2,1,0:T(8,128)(2,1)S(1)}) fusion(f32[32,2,512]{2,0,1:T(8,128)S(1)} %get-tuple-element.97, f32[64,2,512]{2,1,0:T(2,128)S(1)} %get-tuple-element.98, f32[32,2,512]{2,0,1:T(8,128)S(1)} %get-tuple-element.99, f32[64,2,512]{2,1,0:T(2,128)S(1)} %get-tuple-element.100), kind=kLoop, calls=%fused_computation.2.clone.1 | loop fusion | flops 14680064 | bytes 4980736 | tf_op jit(solution)/shard_map/while/body/eval_jaxpr/reduce_sum | solution.py:51
  165.6 2.2 %fusion.55 = bf16[8,64,32,256]{3,2,1,0:T(8,128)(2,1)} fusion(bf16[8,64,32,256]{3,2,1,0:T(8,128)(2,1)} %get-tuple-element.110, s32[]{:T(128)} %get-tuple-element.109, bf16[64,32,512]{2,1,0:T(8,128)(2,1)S(1)} %get-tuple-element.101, bf16[64,32,512]{2,1,0:T(8,128)(2,1)S(1)} %get-tuple-element.102, bf16[1024,256]{1,0:T(8,128)(2,1)S(1)} %get-tuple-element.119), kind=kOutput, calls=%fused_computation.9.clone.1 | convolution fusion | flops 1082654720 | bytes 5767680 | tf_op jit(solution)/shard_map/while/body/eval_jaxpr/dot_general | solution.py:56
  168.1 5.4 %add_reduce_fusion.2 = (bf16[64,32,512]{2,1,0:T(8,128)(2,1)S(1)}, bf16[64,32,512]{2,1,0:T(8,128)(2,1)S(1)}) fusion(f32[32,2,512]{2,0,1:T(8,128)S(1)} %get-tuple-element.97, f32[64,2,512]{2,1,0:T(2,128)S(1)} %get-tuple-element.98, f32[32,2,512]{2,0,1:T(8,128)S(1)} %get-tuple-element.99, f32[64,2,512]{2,1,0:T(2,128)S(1)} %get-tuple-element.100), kind=kLoop, calls=%fused_computation.2.clone.1 | loop fusion | flops 14680064 | bytes 4980736 | tf_op jit(solution)/shard_map/while/body/eval_jaxpr/reduce_sum | solution.py:51
  173.5 2.2 %fusion.55 = bf16[8,64,32,256]{3,2,1,0:T(8,128)(2,1)} fusion(bf16[8,64,32,256]{3,2,1,0:T(8,128)(2,1)} %get-tuple-element.110, s32[]{:T(128)} %get-tuple-element.109, bf16[64,32,512]{2,1,0:T(8,128)(2,1)S(1)} %get-tuple-element.101, bf16[64,32,512]{2,1,0:T(8,128)(2,1)S(1)} %get-tuple-element.102, bf16[1024,256]{1,0:T(8,128)(2,1)S(1)} %get-tuple-element.119), kind=kOutput, calls=%fused_computation.9.clone.1 | convolution fusion | flops 1082654720 | bytes 5767680 | tf_op jit(solution)/shard_map/while/body/eval_jaxpr/dot_general | solution.py:56
  176.0 5.4 %add_reduce_fusion.2 = (bf16[64,32,512]{2,1,0:T(8,128)(2,1)S(1)}, bf16[64,32,512]{2,1,0:T(8,128)(2,1)S(1)}) fusion(f32[32,2,512]{2,0,1:T(8,128)S(1)} %get-tuple-element.97, f32[64,2,512]{2,1,0:T(2,128)S(1)} %get-tuple-element.98, f32[32,2,512]{2,0,1:T(8,128)S(1)} %get-tuple-element.99, f32[64,2,512]{2,1,0:T(2,128)S(1)} %get-tuple-element.100), kind=kLoop, calls=%fused_computation.2.clone.1 | loop fusion | flops 14680064 | bytes 4980736 | tf_op jit(solution)/shard_map/while/body/eval_jaxpr/reduce_sum | solution.py:51
  181.4 2.2 %fusion.55 = bf16[8,64,32,256]{3,2,1,0:T(8,128)(2,1)} fusion(bf16[8,64,32,256]{3,2,1,0:T(8,128)(2,1)} %get-tuple-element.110, s32[]{:T(128)} %get-tuple-element.109, bf16[64,32,512]{2,1,0:T(8,128)(2,1)S(1)} %get-tuple-element.101, bf16[64,32,512]{2,1,0:T(8,128)(2,1)S(1)} %get-tuple-element.102, bf16[1024,256]{1,0:T(8,128)(2,1)S(1)} %get-tuple-element.119), kind=kOutput, calls=%fused_computation.9.clone.1 | convolution fusion | flops 1082654720 | bytes 5767680 | tf_op jit(solution)/shard_map/while/body/eval_jaxpr/dot_general | solution.py:56
  183.9 5.4 %add_reduce_fusion.2 = (bf16[64,32,512]{2,1,0:T(8,128)(2,1)S(1)}, bf16[64,32,512]{2,1,0:T(8,128)(2,1)S(1)}) fusion(f32[32,2,512]{2,0,1:T(8,128)S(1)} %get-tuple-element.97, f32[64,2,512]{2,1,0:T(2,128)S(1)} %get-tuple-element.98, f32[32,2,512]{2,0,1:T(8,128)S(1)} %get-tuple-element.99, f32[64,2,512]{2,1,0:T(2,128)S(1)} %get-tuple-element.100), kind=kLoop, calls=%fused_computation.2.clone.1 | loop fusion | flops 14680064 | bytes 4980736 | tf_op jit(solution)/shard_map/while/body/eval_jaxpr/reduce_sum | solution.py:51
  189.3 2.2 %fusion.55 = bf16[8,64,32,256]{3,2,1,0:T(8,128)(2,1)} fusion(bf16[8,64,32,256]{3,2,1,0:T(8,128)(2,1)} %get-tuple-element.110, s32[]{:T(128)} %get-tuple-element.109, bf16[64,32,512]{2,1,0:T(8,128)(2,1)S(1)} %get-tuple-element.101, bf16[64,32,512]{2,1,0:T(8,128)(2,1)S(1)} %get-tuple-element.102, bf16[1024,256]{1,0:T(8,128)(2,1)S(1)} %get-tuple-element.119), kind=kOutput, calls=%fused_computation.9.clone.1 | convolution fusion | flops 1082654720 | bytes 5767680 | tf_op jit(solution)/shard_map/while/body/eval_jaxpr/dot_general | solution.py:56
  191.8 5.4 %add_reduce_fusion.2 = (bf16[64,32,512]{2,1,0:T(8,128)(2,1)S(1)}, bf16[64,32,512]{2,1,0:T(8,128)(2,1)S(1)}) fusion(f32[32,2,512]{2,0,1:T(8,128)S(1)} %get-tuple-element.97, f32[64,2,512]{2,1,0:T(2,128)S(1)} %get-tuple-element.98, f32[32,2,512]{2,0,1:T(8,128)S(1)} %get-tuple-element.99, f32[64,2,512]{2,1,0:T(2,128)S(1)} %get-tuple-element.100), kind=kLoop, calls=%fused_computation.2.clone.1 | loop fusion | flops 14680064 | bytes 4980736 | tf_op jit(solution)/shard_map/while/body/eval_jaxpr/reduce_sum | solution.py:51
  197.3 2.2 %fusion.55 = bf16[8,64,32,256]{3,2,1,0:T(8,128)(2,1)} fusion(bf16[8,64,32,256]{3,2,1,0:T(8,128)(2,1)} %get-tuple-element.110, s32[]{:T(128)} %get-tuple-element.109, bf16[64,32,512]{2,1,0:T(8,128)(2,1)S(1)} %get-tuple-element.101, bf16[64,32,512]{2,1,0:T(8,128)(2,1)S(1)} %get-tuple-element.102, bf16[1024,256]{1,0:T(8,128)(2,1)S(1)} %get-tuple-element.119), kind=kOutput, calls=%fused_computation.9.clone.1 | convolution fusion | flops 1082654720 | bytes 5767680 | tf_op jit(solution)/shard_map/while/body/eval_jaxpr/dot_general | solution.py:56
  (45 shorter events, 5.4 us)
Async XLA Ops:
  1.9 19.3 %all-to-all-start = ((bf16[32,2,1024]{2,1,0:T(2,128)(2,1)}), bf16[32,2,1024]{2,1,0:T(2,128)(2,1)S(1)}, u32[]{:S(2)}, u32[]{:S(2)}) async-start(bf16[32,2,1024]{2,1,0:T(2,128)(2,1)} %reshape.91), calls=%async_computation | async-start | bytes 262144 | tf_op jit(solution)/shard_map/all_to_all | solution.py:72
where the time goes:
time: 201 us; the launch traced here: 199 us
  blocking collectives  92.4 us (46%)
  other arithmetic  61.3 us (30%)
  local copies, waits for them, and re-layouts  19.4 us (10%)
  matrix products  18.3 us (9%)
  starting transfers between devices  7.1 us (4%)
    psum x1, blocking collectives, on_device(): band = lax.psum(picked, 'col').astype(jnp.bfloat16)  92.4 us
    reduce_sum x8, other arithmetic, correlate_block(): cross_real = jnp.sum(row_real * col_real + row_imag * col_imag, axis=2)  43.4 us
    dot_general x8, matrix products, correlate_block(): jnp.dot(cross.reshape(rows_here * cols_here, 2 * F), inverse, preferred_e...  17.8 us
    gather x1, local copies, waits for them, and re-layouts, on_device(): jnp.take(white, jnp.clip(offsets, 0, block_channels - 1), axis=0)  16.3 us
    another operation x1, other arithmetic  8.54 us
    all_to_all x1, starting transfers between devices, on_device(): lax.all_to_all(records, 'col', split_axis=0, concat_axis=1, tiled=True)  7.1 us
    mul x1, other arithmetic, on_device(): picked = picked * inside[:, None, None]  4.32 us
  transfers between devices with their start and end apart: 1, of which 0 were waited for; matrix products, arithmetic and copies ran while one was open for 6% of the time, Pallas kernels for 0%

commit v1 on v0

v1 whole, which is shorter than its diff:
```python
import functools

import jax
import jax.numpy as jnp
import numpy as np
from jax import lax
from jax.experimental import pallas as pl
from jax.experimental.pallas import tpu as pltpu
from jax.sharding import PartitionSpec as P

L = 1024
LAGS = 256
SEG = 2
ROWS = 512
F = 512
SUB = 8


def dft_tables():
    t = np.arange(L)
    f = np.arange(F)
    phase = np.mod(t[:, None] * f[None, :], L) * (2.0 * np.pi / L)
    forward = np.concatenate([np.cos(phase), -np.sin(phase)], axis=1).astype(np.float32)
    shifts = np.arange(LAGS) - LAGS // 2
    turns = np.mod(f[:, None] * shifts[None, :], L) * (2.0 * np.pi / L)
    inverse = np.concatenate([np.cos(turns), -np.sin(turns)], axis=0) / np.sqrt(SEG * F)
    return forward.astype(jnp.bfloat16), inverse.astype(np.float32).astype(jnp.bfloat16)


def whiten(sp0, sp1, keep):
    re0, im0, re1, im1 = sp0[:, :F], sp0[:, F:], sp1[:, :F], sp1[:, F:]
    power = ((re0 * re0 + im0 * im0) + (re1 * re1 + im1 * im1)) * (1.0 / SEG)
    level = jnp.mean(power, axis=1, keepdims=True)
    scale = lax.rsqrt(power + level + 1e-06) * keep
    return [(part * scale).astype(jnp.bfloat16) for part in (re0, im0, re1, im1)]


def correlate_kernel(
    channels, xb_ref, xo_ref, kb_ref, ko_ref, fwd_ref, inv_ref, out_ref,
    wb, wo, cross_a, cross_b, out_buf, sems,
):
    groups = channels // 16
    dot0 = functools.partial(
        lax.dot_general, dimension_numbers=(((0,), (0,)), ((), ())),
        preferred_element_type=jnp.float32,
    )
    own = [
        jnp.dot(xo_ref[:, s * L:(s + 1) * L], fwd_ref[...], preferred_element_type=jnp.float32)
        for s in range(SEG)
    ]
    for q, part in enumerate(whiten(own[0], own[1], ko_ref[...])):
        wo[:, q * F:(q + 1) * F] = part

    width = 256

    @pl.loop(0, ROWS // width)
    def _(i):
        cols = pl.ds(pl.multiple_of(i * width, width), width)
        band = [dot0(xb_ref[s * L:(s + 1) * L, cols], fwd_ref[...]) for s in range(SEG)]
        for q, part in enumerate(whiten(band[0], band[1], kb_ref[cols, :])):
            wb[cols, q * F:(q + 1) * F] = part.astype(jnp.float32)

    def cross(base, buf):
        for j in range(F // 128):
            lanes = [slice(q * F + j * 128, q * F + (j + 1) * 128) for q in range(4)]
            cols = [[wo[g * 16:(g + 1) * 16, lane] for lane in lanes] for g in range(groups)]
            rows8 = [wb[pl.ds(pl.multiple_of(base, SUB), SUB), lane] for lane in lanes]
            for i in range(SUB):
                a0, b0, a1, b1 = [
                    jnp.broadcast_to(tile[i:i + 1, :], (16, 128)).astype(jnp.bfloat16)
                    for tile in rows8
                ]
                for g in range(groups):
                    c0, d0, c1, d1 = cols[g]
                    real = (a0 * c0 + b0 * d0) + (a1 * c1 + b1 * d1)
                    imag = (b0 * c0 - a0 * d0) + (b1 * c1 - a1 * d1)
                    rows = slice(i * channels + g * 16, i * channels + (g + 1) * 16)
                    buf[rows, j * 128:(j + 1) * 128] = real
                    buf[rows, F + j * 128:F + (j + 1) * 128] = imag

    def lags(base, buf):
        res = jnp.dot(buf[...], inv_ref[...], preferred_element_type=jnp.float32)
        out_buf[pl.ds(pl.multiple_of(base, SUB), SUB)] = res.astype(jnp.bfloat16).reshape(SUB, channels, LAGS)

    def copy_out(k):
        rows = pl.ds(k * 2 * SUB, 2 * SUB)
        return pltpu.make_async_copy(out_buf.at[rows], out_ref.at[rows], sems.at[k])

    steps = ROWS // (2 * SUB)
    cross(0, cross_a)

    @pl.loop(0, steps)
    def _(k):
        base = k * 2 * SUB
        lags(base, cross_a)
        cross(base + SUB, cross_b)
        lags(base + SUB, cross_b)
        cross(jnp.minimum(base + 2 * SUB, ROWS - SUB), cross_a)
        copy_out(k).start()

    @pl.loop(0, steps)
    def _(k):
        copy_out(k).wait()


def on_device(records, quality_mask, band_start):
    devices_col = lax.axis_size("col")
    position = lax.axis_index("col")
    channels = records.shape[0] // devices_col
    forward, inverse = dft_tables()
    first_row = band_start[0]
    slab = lax.dynamic_slice_in_dim(records.T, first_row, ROWS, 1)
    band = lax.all_gather(slab, "col", axis=0, tiled=True)
    own = lax.all_to_all(records, "col", split_axis=0, concat_axis=1, tiled=True)
    mask = quality_mask.astype(jnp.float32)
    keep_band = lax.dynamic_slice_in_dim(mask, first_row, ROWS, 0)[:, None]
    keep_own = lax.dynamic_slice_in_dim(mask, position * channels, channels, 0)[:, None]
    vmem = pl.BlockSpec(memory_space=pltpu.VMEM)
    return pl.pallas_call(
        functools.partial(correlate_kernel, channels),
        out_shape=jax.ShapeDtypeStruct((ROWS, channels, LAGS), jnp.bfloat16),
        in_specs=[vmem] * 6,
        out_specs=pl.BlockSpec(memory_space=pl.ANY),
        scratch_shapes=[
            pltpu.VMEM((ROWS, 4 * F), jnp.float32),
            pltpu.VMEM((channels, 4 * F), jnp.bfloat16),
            pltpu.VMEM((SUB * channels, 2 * F), jnp.bfloat16),
            pltpu.VMEM((SUB * channels, 2 * F), jnp.bfloat16),
            pltpu.VMEM((ROWS, channels, LAGS), jnp.bfloat16),
            pltpu.SemaphoreType.DMA((ROWS // (2 * SUB),)),
        ],
        compiler_params=pltpu.CompilerParams(vmem_limit_bytes=52 * 2**20),
    )(band, own, keep_band, keep_own, jnp.asarray(forward), jnp.asarray(inverse))


def solution(mesh):
    return jax.shard_map(
        on_device,
        mesh=mesh,
        in_specs=(P("win", "col"), P("win"), P("win")),
        out_specs=P("win", "col", None),
        check_vma=False,
    )
```

time: 201 us -> 106 us (0.53)
  blocking collectives: 92.4 us -> 0 us
  other arithmetic: 61.3 us -> 0.69 us
  waiting for transfers between devices: 0.01 us -> 49.5 us
  Pallas kernels: 0 us -> 29.1 us
  matrix products: 18.3 us -> 0 us
  local copies, waits for them, and re-layouts: 19.4 us -> 4.51 us
  between operations: 0.81 us -> 14.2 us
    psum x1 -> x0, blocking collectives: 92.4 us -> none  [on_device(): band = lax.psum(picked, 'col').astype(jnp.bfloat16)]
    reduce_sum x10 -> x0, other arithmetic: 43.8 us -> none  [the longest x8 43.4 us: correlate_block(): cross_real = jnp.sum(row_real * col_real + row_imag * col_imag, axis=2)]
    all_gather x0 -> x1, waiting for transfers between devices: none -> 42.4 us  [on_device(): band = lax.all_gather(slab, 'col', axis=0, tiled=True)]
    pallas_call x0 -> x1, Pallas kernels: none -> 29.1 us  [on_device(): pl.pallas_call(functools.partial(correlate_kernel, channels), out_shape=j...]
    dot_general x9 -> x0, matrix products: 18.3 us -> none  [the longest x8 17.8 us: correlate_block(): jnp.dot(cross.reshape(rows_here * cols_here, 2 * F), inverse, preferred_e...]
    gather x1 -> x0, local copies, waits for them, and re-layouts: 16.3 us -> none  [on_device(): jnp.take(white, jnp.clip(offsets, 0, block_channels - 1), axis=0)]
    another operation x1 -> x0, other arithmetic: 8.54 us -> none
    all_to_all x1, waiting for transfers between devices: 0.01 us -> 7.1 us  [on_device(): lax.all_to_all(records, 'col', split_axis=0, concat_axis=1, tiled=True)]
  transfers between devices with their start and end apart: 1 -> 2, of which waited for: 0 -> 2; matrix products, arithmetic and copies ran while one was open for 6% -> 3% of each run, Pallas kernels for 0% -> 0%
where the time goes in v1:
time: 106 us; the launch traced here: 105 us
  waiting for transfers between devices  49.5 us (47%)
  Pallas kernels  29.1 us (27%)
  between operations  14.2 us (13%)
  starting transfers between devices  7.1 us (7%)
  local copies, waits for them, and re-layouts  4.51 us (4%)
    all_gather x1, waiting for transfers between devices, on_device(): band = lax.all_gather(slab, 'col', axis=0, tiled=True)  42.4 us
    pallas_call x1, Pallas kernels, on_device(): pl.pallas_call(functools.partial(correlate_kernel, channels), out_shape=j...  29.1 us
    all_to_all x1, waiting for transfers between devices, on_device(): lax.all_to_all(records, 'col', split_axis=0, concat_axis=1, tiled=True)  7.1 us
    all_to_all x1, starting transfers between devices, on_device(): lax.all_to_all(records, 'col', split_axis=0, concat_axis=1, tiled=True)  7.1 us
    unnamed x5, local copies, waits for them, and re-layouts  2.15 us
  transfers between devices with their start and end apart: 2, of which 2 were waited for; matrix products, arithmetic and copies ran while one was open for 3% of the time, Pallas kernels for 0%

profile of v1, /device:TPU:1, one launch (start us, length us, event | category | flops | bytes accessed | tf_op | source)
XLA Modules:
  0.0 105.1 jit_solution(17310052843911488550)
XLA Ops:
  6.5 0.0 copy-start
  6.5 0.0 all-gather.2.cloned.1.call-start
  7.3 1.6 %dynamic-slice_bitcast_fusion = bf16[64,512]{1,0:T(8,128)(2,1)} fusion(bf16[1024,64]{0,1:T(8,128)(2,1)} %param.5, s32[]{:T(128)S(6)} %select_n.7), kind=kLoop, calls=%fused_computation | loop fusion | bytes 131076 | tf_op jit(solution)/shard_map/dynamic_slice | solution.py:112
  8.9 0.0 all-gather.2.cloned.1.call-update
  8.9 1.1 %copy.8 = bf16[1024,64]{1,0:T(8,128)(2,1)S(1)} copy(bf16[1024,64]{0,1:T(8,128)(2,1)} %param.5) | data formatting | bytes 262144 | tf_op args[0]
  10.0 0.9 reshape.3
  10.8 7.1 %all-to-all-start = ((bf16[32,2,1024]{2,1,0:T(2,128)(2,1)}), bf16[32,2,1024]{2,1,0:T(2,128)(2,1)S(1)}, u32[]{:S(2)}, u32[]{:S(2)}) async-start(bf16[32,2,1024]{2,1,0:T(2,128)(2,1)} %reshape.3), calls=%async_computation | async-start | bytes 262144 | tf_op jit(solution)/shard_map/all_to_all | solution.py:114
  17.9 0.7 convert_element_type.3
  18.6 0.1 dynamic_slice.10
  18.7 0.1 dynamic-slice_bitcast_fusion.1
  18.8 0.1 copy.11.ko_ref
  18.9 0.1 copy.10.kb_ref
  19.0 7.1 %all-to-all-done = bf16[32,2,1024]{2,1,0:T(2,128)(2,1)S(1)} async-done(((bf16[32,2,1024]{2,1,0:T(2,128)(2,1)}), bf16[32,2,1024]{2,1,0:T(2,128)(2,1)S(1)}, u32[]{:S(2)}, u32[]{:S(2)}) %all-to-all-start) | async-done | bytes 131104 | tf_op jit(solution)/shard_map/all_to_all | solution.py:114
  26.1 0.2 reshape.4
  26.3 0.1 copy.9
  26.5 0.3 all_to_all.17.xo_ref
  26.7 42.4 %all-gather.2.cloned.1.call-done.xb_ref = bf16[2048,512]{1,0:T(8,128)(2,1)} async-done(((bf16[64,512]{1,0:T(8,128)(2,1)}), bf16[2048,512]{1,0:T(8,128)(2,1)}) %all-gather.2.cloned.1.call-update) | async-done | bytes 2097168 | tf_op jit(solution)/shard_map/all_gather | solution.py:113
  69.1 0.0 copy-done
  69.1 29.1 %shard_map.55 = bf16[512,32,256]{2,1,0:T(8,128)(2,1)} custom-call(bf16[2048,512]{1,0:T(8,128)(2,1)} %all-gather.2.cloned.1.call-done.xb_ref, bf16[32,2048]{1,0:T(8,128)(2,1)S(1)} %all_to_all.17.xo_ref, f32[512,1]{1,0:T(8,128)S(1)} %copy.10.kb_ref, f32[32,1]{1,0:T(8,128)S(1)} %copy.11.ko_ref, bf16[1024,1024]{1,0:T(8,128)(2,1)} %constant.14.clone.fwd_ref, ...), custom_call_target="tpu_custom_call" | custom-call | tf_op jit(solution)/shard_map/pallas_call | solution.py:119
Async XLA Ops:
  6.5 62.6 %copy-start = (bf16[1024,256]{1,0:T(8,128)(2,1)S(1)}, bf16[1024,256]{1,0:T(8,128)(2,1)}, u32[]{:S(2)}) copy-start(bf16[1024,256]{1,0:T(8,128)(2,1)} %constant.15.clone.inv_ref) | copy-start | bytes 1572868
  6.5 62.6 %all-gather.2.cloned.1.call-start = ((), (), s32[]{:S(2)}) async-start(), calls=%async_computation.1 | async-start | bytes 2162688 | tf_op jit(solution)/shard_map/all_gather | solution.py:113
  10.8 15.3 %all-to-all-start = ((bf16[32,2,1024]{2,1,0:T(2,128)(2,1)}), bf16[32,2,1024]{2,1,0:T(2,128)(2,1)S(1)}, u32[]{:S(2)}, u32[]{:S(2)}) async-start(bf16[32,2,1024]{2,1,0:T(2,128)(2,1)} %reshape.3), calls=%async_computation | async-start | bytes 262144 | tf_op jit(solution)/shard_map/all_to_all | solution.py:114
Sparse Core Ops, SparseCore 0:
  10.2 58.8 all-gather.1

commit v2 on v1

--- a/solution.py
+++ b/solution.py
@@ -35,6 +35,142 @@
     return [(part * scale).astype(jnp.bfloat16) for part in (re0, im0, re1, im1)]
 
 
+def prep_kernel(channels, groups, start_ref, rec_ref, slab_ref, pack_ref):
+    total = rec_ref.shape[1]
+    rec = rec_ref[...].astype(jnp.float32)
+    shifted = pltpu.roll(rec, lax.rem(total - start_ref[0], total), 1)
+    for h in range(2):
+        slab_ref[h] = shifted[:, h * ROWS // 2:(h + 1) * ROWS // 2].astype(jnp.bfloat16)
+    lane = lax.broadcasted_iota(jnp.int32, (16, 128), 1)
+    per_tile = 128 // channels
+    for dest in range(total // channels):
+        j, i = divmod(dest, per_tile)
+        packed = jnp.zeros((16, 128), jnp.float32)
+        for k in range(groups):
+            piece = rec[16 * k:16 * (k + 1), 128 * j:128 * (j + 1)]
+            if k != i:
+                piece = pltpu.roll(piece, (channels * (k - i)) % 128, 1)
+            inside = (lane >= channels * k) & (lane < channels * (k + 1))
+            packed = jnp.where(inside, piece, packed)
+        pack_ref[dest] = packed.astype(jnp.bfloat16)
+
+
+def bit_orders(n):
+    bits = [1 << b for b in range(n.bit_length() - 1)]
+    down = bits[::-1]
+    other = list(down)
+    if len(bits) >= 4:
+        other[-3], other[-2] = other[-2], other[-3]
+    return down, other
+
+
+def exchange_kernel(
+    n, slab_ref, pack_ref, gath_ref, own_ref,
+    send_sems, recv_sems, own_send, own_recv, local_sems,
+):
+    me = lax.axis_index("col")
+
+    def flip(mask):
+        index = me
+        for b in range(n.bit_length()):
+            if mask >> b & 1:
+                index = index + (1 << b) * (1 - 2 * ((me // (1 << b)) % 2))
+        return index
+
+    barrier = pltpu.get_barrier_semaphore()
+
+    @pl.loop(1, n)
+    def _(d):
+        pl.semaphore_signal(
+            barrier, inc=1, device_id={"col": (me + d) % n}, device_id_type=pl.DeviceIdType.MESH
+        )
+
+    pl.semaphore_wait(barrier, n - 1)
+
+    def piece(h, held, bit):
+        slot = gath_ref.at[h, flip(held)]
+        return pltpu.make_async_remote_copy(
+            src_ref=slab_ref.at[h] if held == 0 else slot,
+            dst_ref=slot,
+            send_sem=send_sems.at[h, held ^ bit],
+            recv_sem=recv_sems.at[h, held ^ bit],
+            device_id={"col": flip(bit)},
+            device_id_type=pl.DeviceIdType.MESH,
+        )
+
+    def arrival(h, mask):
+        slot = gath_ref.at[h, flip(mask)]
+        return pltpu.make_async_remote_copy(
+            src_ref=slab_ref.at[h],
+            dst_ref=slot,
+            send_sem=send_sems.at[h, mask],
+            recv_sem=recv_sems.at[h, mask],
+            device_id={"col": flip(1)},
+            device_id_type=pl.DeviceIdType.MESH,
+        )
+
+    def own_push(d):
+        return pltpu.make_async_remote_copy(
+            src_ref=pack_ref.at[(me + d) % n],
+            dst_ref=own_ref.at[me],
+            send_sem=own_send.at[d],
+            recv_sem=own_recv.at[d],
+            device_id={"col": (me + d) % n},
+            device_id_type=pl.DeviceIdType.MESH,
+        )
+
+    def own_arrival(d):
+        return pltpu.make_async_remote_copy(
+            src_ref=pack_ref.at[0],
+            dst_ref=own_ref.at[(me - d + n) % n],
+            send_sem=own_send.at[d],
+            recv_sem=own_recv.at[d],
+            device_id={"col": (me + d) % n},
+            device_id_type=pl.DeviceIdType.MESH,
+        )
+
+    local = [pltpu.make_async_copy(slab_ref.at[h], gath_ref.at[h, me], local_sems.at[h]) for h in range(2)]
+    local.append(pltpu.make_async_copy(pack_ref.at[me], own_ref.at[me], local_sems.at[2]))
+
+    orders = bit_orders(n)
+    held = [[0], [0]]
+    waited = [set(), set()]
+    started = []
+    for stage in range(len(orders[0])):
+        for pos in range(len(held[0])):
+            for h in range(2):
+                mask, bit = held[h][pos], orders[h][stage]
+                if mask and mask not in waited[h]:
+                    arrival(h, mask).wait_recv()
+                    waited[h].add(mask)
+                copy = piece(h, mask, bit)
+                copy.start()
+                started.append(copy)
+        for h in range(2):
+            held[h] = held[h] + [mask ^ orders[h][stage] for mask in held[h]]
+        if stage == 0:
+            for copy in local:
+                copy.start()
+
+            @pl.loop(1, n)
+            def _(d):
+                own_push(d).start()
+
+    for h in range(2):
+        for mask in held[h]:
+            if mask and mask not in waited[h]:
+                arrival(h, mask).wait_recv()
+    for copy in started:
+        copy.wait_send()
+    for copy in local:
+        copy.wait()
+
+    @pl.loop(1, n)
+    def _(d):
+        own_push(d).wait_send()
+        own_arrival(d).wait_recv()
+
+
 def correlate_kernel(
     channels, xb_ref, xo_ref, kb_ref, ko_ref, fwd_ref, inv_ref, out_ref,
     wb, wo, cross_a, cross_b, out_buf, sems,
@@ -44,19 +180,24 @@
         lax.dot_general, dimension_numbers=(((0,), (0,)), ((), ())),
         preferred_element_type=jnp.float32,
     )
-    own = [
-        jnp.dot(xo_ref[:, s * L:(s + 1) * L], fwd_ref[...], preferred_element_type=jnp.float32)
-        for s in range(SEG)
-    ]
+    half = xo_ref.shape[0] // SEG
+    table = fwd_ref[...].reshape(half, L // half, 2 * F)
+    own = []
+    for s in range(SEG):
+        samples = xo_ref[s * half:(s + 1) * half].reshape(half * 16, 128)
+        own.append(jnp.zeros((channels, 2 * F), jnp.float32))
+        for k in range(L // half // 16):
+            rows = table[:, 16 * k:16 * (k + 1), :].reshape(half * 16, 2 * F)
+            own[s] += dot0(samples, rows)[channels * k:channels * (k + 1)]
     for q, part in enumerate(whiten(own[0], own[1], ko_ref[...])):
         wo[:, q * F:(q + 1) * F] = part
 
-    width = 256
-
-    @pl.loop(0, ROWS // width)
+    width = ROWS // 2
+
+    @pl.loop(0, 2)
     def _(i):
         cols = pl.ds(pl.multiple_of(i * width, width), width)
-        band = [dot0(xb_ref[s * L:(s + 1) * L, cols], fwd_ref[...]) for s in range(SEG)]
+        band = [dot0(xb_ref[i, s * L:(s + 1) * L, :], fwd_ref[...]) for s in range(SEG)]
         for q, part in enumerate(whiten(band[0], band[1], kb_ref[cols, :])):
             wb[cols, q * F:(q + 1) * F] = part.astype(jnp.float32)
 
@@ -109,13 +250,41 @@
     channels = records.shape[0] // devices_col
     forward, inverse = dft_tables()
     first_row = band_start[0]
-    slab = lax.dynamic_slice_in_dim(records.T, first_row, ROWS, 1)
-    band = lax.all_gather(slab, "col", axis=0, tiled=True)
-    own = lax.all_to_all(records, "col", split_axis=0, concat_axis=1, tiled=True)
+    local_time = records.shape[1]
+    groups = local_time // 16
+    n = devices_col
+    vmem = pl.BlockSpec(memory_space=pltpu.VMEM)
+    hbm = pl.BlockSpec(memory_space=pl.ANY)
+    slab, pack = pl.pallas_call(
+        functools.partial(prep_kernel, channels, groups),
+        out_shape=(
+            jax.ShapeDtypeStruct((2, local_time, ROWS // 2), jnp.bfloat16),
+            jax.ShapeDtypeStruct((n, 16, 128), jnp.bfloat16),
+        ),
+        in_specs=[pl.BlockSpec(memory_space=pltpu.SMEM), vmem],
+        out_specs=(vmem, vmem),
+    )(band_start, records.T)
+    band, own = pl.pallas_call(
+        functools.partial(exchange_kernel, n),
+        out_shape=(
+            jax.ShapeDtypeStruct((2, n, local_time, ROWS // 2), jnp.bfloat16),
+            jax.ShapeDtypeStruct((n, 16, 128), jnp.bfloat16),
+        ),
+        in_specs=[hbm, hbm],
+        out_specs=(hbm, hbm),
+        scratch_shapes=[
+            pltpu.SemaphoreType.DMA((2, n)),
+            pltpu.SemaphoreType.DMA((2, n)),
+            pltpu.SemaphoreType.DMA((n,)),
+            pltpu.SemaphoreType.DMA((n,)),
+            pltpu.SemaphoreType.DMA((3,)),
+        ],
+        compiler_params=pltpu.CompilerParams(collective_id=0, has_side_effects=True),
+    )(slab, pack)
+    band = band.reshape(2, n * local_time, ROWS // 2)
     mask = quality_mask.astype(jnp.float32)
     keep_band = lax.dynamic_slice_in_dim(mask, first_row, ROWS, 0)[:, None]
     keep_own = lax.dynamic_slice_in_dim(mask, position * channels, channels, 0)[:, None]
-    vmem = pl.BlockSpec(memory_space=pltpu.VMEM)
     return pl.pallas_call(
         functools.partial(correlate_kernel, channels),
         out_shape=jax.ShapeDtypeStruct((ROWS, channels, LAGS), jnp.bfloat16),

time: 106 us -> 61.3 us (0.58)
  waiting for transfers between devices: 49.5 us -> 0 us
  Pallas kernels: 29.1 us -> 57.4 us
  between operations: 14.2 us -> 0.69 us
  starting transfers between devices: 7.1 us -> 0 us
  local copies, waits for them, and re-layouts: 4.51 us -> 2.32 us
    all_gather x1 -> x0, waiting for transfers between devices: 42.4 us -> none  [on_device(): band = lax.all_gather(slab, 'col', axis=0, tiled=True)]
    pallas_call x0 -> x2, Pallas kernels: none -> 28.4 us  [the longest x1 26.6 us: on_device(): pl.pallas_call(functools.partial(exchange_kernel, n), out_shape=(jax.Shap...]
    all_to_all x1 -> x0, waiting for transfers between devices: 7.1 us -> none  [on_device(): lax.all_to_all(records, 'col', split_axis=0, concat_axis=1, tiled=True)]
    all_to_all x1 -> x0, starting transfers between devices: 7.1 us -> none  [on_device(): lax.all_to_all(records, 'col', split_axis=0, concat_axis=1, tiled=True)]
    dynamic_slice x1 -> x0, local copies, waits for them, and re-layouts: 1.6 us -> none  [on_device(): slab = lax.dynamic_slice_in_dim(records.T, first_row, ROWS, 1)]
    unnamed x5 -> x4, local copies, waits for them, and re-layouts: 2.15 us -> 1.94 us
  transfers between devices with their start and end apart: 2 -> 0, of which waited for: 2 -> 0; matrix products, arithmetic and copies ran while one was open for 3% -> 0% of each run, Pallas kernels for 0% -> 0%
where the time goes in v2:
time: 61.3 us; the launch traced here: 61.1 us
  Pallas kernels  57.4 us (94%)
  local copies, waits for them, and re-layouts  2.32 us (4%)
  other arithmetic  0.69 us (1%)
  between operations  0.69 us (1%)
    pallas_call x1, Pallas kernels, on_device(): pl.pallas_call(functools.partial(correlate_kernel, channels), out_shape=j...  29 us
    pallas_call x1, Pallas kernels, on_device(): pl.pallas_call(functools.partial(exchange_kernel, n), out_shape=(jax.Shap...  26.6 us
    unnamed x4, local copies, waits for them, and re-layouts  1.94 us
    pallas_call x1, Pallas kernels, on_device(): pl.pallas_call(functools.partial(prep_kernel, channels, groups), out_shap...  1.77 us

profile of v2, /device:TPU:1, one launch (start us, length us, event | category | flops | bytes accessed | tf_op | source)
XLA Modules:
  0.0 61.1 jit_solution(16281362870420268276)
XLA Ops:
  0.7 0.7 %convert_element_type.3 = f32[1024]{0:T(1024)S(1)} convert(s32[1024]{0:T(1024)} %param.6) | non-fusion elementwise | flops 1024 | bytes 8192 | tf_op jit(solution)/shard_map/convert_element_type | solution.py:285
  1.3 0.1 dynamic-slice_bitcast_fusion
  1.4 0.1 dynamic_slice.6
  1.5 0.1 copy.8.ko_ref
  1.6 1.8 %shard_map.55 = (bf16[2,64,256]{2,1,0:T(8,128)(2,1)}, bf16[32,16,128]{2,1,0:T(8,128)(2,1)}) custom-call(s32[1]{0:T(128)} %copy.9.start_ref, bf16[64,1024]{1,0:T(8,128)(2,1)} %bitcast.10), custom_call_target="tpu_custom_call" | custom-call | tf_op jit(solution)/shard_map/pallas_call | solution.py:258
  3.4 0.1 copy.7.kb_ref
  3.5 26.6 %shard_map.56 = (bf16[2,32,64,256]{3,2,1,0:T(8,128)(2,1)}, bf16[32,16,128]{2,1,0:T(8,128)(2,1)}) custom-call(bf16[2,64,256]{2,1,0:T(8,128)(2,1)} %get-tuple-element.9.slab_ref, bf16[32,16,128]{2,1,0:T(8,128)(2,1)} %get-tuple-element.10.pack_ref), custom_call_target="tpu_custom_call" | custom-call | tf_op jit(solution)/shard_map/pallas_call | solution.py:267
  30.1 0.0 copy-start
  30.1 1.0 %copy-done = bf16[1024,256]{1,0:T(8,128)(2,1)S(1)} copy-done((bf16[1024,256]{1,0:T(8,128)(2,1)S(1)}, bf16[1024,256]{1,0:T(8,128)(2,1)}, u32[]{:S(2)}) %copy-start) | copy-done | bytes 524312
  31.2 0.0 copy-start.1
  31.2 0.9 %copy-done.1 = bf16[32,16,128]{2,1,0:T(8,128)(2,1)S(1)} copy-done((bf16[32,16,128]{2,1,0:T(8,128)(2,1)S(1)}, bf16[32,16,128]{2,1,0:T(8,128)(2,1)}, u32[]{:S(2)}) %copy-start.1) | copy-done | bytes 131096
  32.1 29.0 %shard_map.57 = bf16[512,32,256]{2,1,0:T(8,128)(2,1)} custom-call(bf16[2,2048,256]{2,1,0:T(8,128)(2,1)} %bitcast.9, bf16[32,16,128]{2,1,0:T(8,128)(2,1)S(1)} %copy-done.1, f32[512,1]{1,0:T(8,128)S(1)} %copy.7.kb_ref, f32[32,1]{1,0:T(8,128)S(1)} %copy.8.ko_ref, bf16[1024,1024]{1,0:T(8,128)(2,1)} %constant.14.clone.fwd_ref, bf16[1024,256]{1,0:T(8,128)(2,1)S(1)} %copy-done), custom_call_target="tpu_custom_call" | custom-call | tf_op jit(solution)/shard_map/pallas_call | solution.py:288
Async XLA Ops:
  30.1 1.0 %copy-start = (bf16[1024,256]{1,0:T(8,128)(2,1)S(1)}, bf16[1024,256]{1,0:T(8,128)(2,1)}, u32[]{:S(2)}) copy-start(bf16[1024,256]{1,0:T(8,128)(2,1)} %constant.15.clone.inv_ref) | copy-start | bytes 1572868
  31.2 0.9 %copy-start.1 = (bf16[32,16,128]{2,1,0:T(8,128)(2,1)S(1)}, bf16[32,16,128]{2,1,0:T(8,128)(2,1)}, u32[]{:S(2)}) copy-start(bf16[32,16,128]{2,1,0:T(8,128)(2,1)} %get-tuple-element.12.xo_ref) | copy-start | bytes 393220

commit v3 on v2

--- a/solution.py
+++ b/solution.py
@@ -13,7 +13,7 @@
 SEG = 2
 ROWS = 512
 F = 512
-SUB = 8
+SUB = 16
 
 
 def dft_tables():
@@ -137,18 +137,19 @@
     waited = [set(), set()]
     started = []
     for stage in range(len(orders[0])):
-        for pos in range(len(held[0])):
-            for h in range(2):
-                mask, bit = held[h][pos], orders[h][stage]
-                if mask and mask not in waited[h]:
-                    arrival(h, mask).wait_recv()
-                    waited[h].add(mask)
+        for h in range(2):
+            held[h] = held[h] + [mask ^ orders[h][stage] for mask in held[h]]
+    for pos in range(n // 2):
+        for h in range(2):
+            mask = held[h][pos]
+            if mask:
+                arrival(h, mask).wait_recv()
+                waited[h].add(mask)
+            for bit in orders[h][pos.bit_length():]:
                 copy = piece(h, mask, bit)
                 copy.start()
                 started.append(copy)
-        for h in range(2):
-            held[h] = held[h] + [mask ^ orders[h][stage] for mask in held[h]]
-        if stage == 0:
+        if pos == 0:
             for copy in local:
                 copy.start()
 
@@ -205,11 +206,11 @@
         for j in range(F // 128):
             lanes = [slice(q * F + j * 128, q * F + (j + 1) * 128) for q in range(4)]
             cols = [[wo[g * 16:(g + 1) * 16, lane] for lane in lanes] for g in range(groups)]
-            rows8 = [wb[pl.ds(pl.multiple_of(base, SUB), SUB), lane] for lane in lanes]
+            tiles = [wb[pl.ds(pl.multiple_of(base, SUB), SUB), lane] for lane in lanes]
             for i in range(SUB):
                 a0, b0, a1, b1 = [
                     jnp.broadcast_to(tile[i:i + 1, :], (16, 128)).astype(jnp.bfloat16)
-                    for tile in rows8
+                    for tile in tiles
                 ]
                 for g in range(groups):
                     c0, d0, c1, d1 = cols[g]

time: 61.3 us -> 57.4 us (0.936)
  Pallas kernels: 57.4 us -> 53.4 us
    pallas_call x1, Pallas kernels: 29 us -> 26.8 us  [on_device(): pl.pallas_call(functools.partial(correlate_kernel, channels), out_shape=j...]
    pallas_call x1, Pallas kernels: 26.6 us -> 24.8 us  [on_device(): pl.pallas_call(functools.partial(exchange_kernel, n), out_shape=(jax.Shap...]
where the time goes in v3:
time: 57.4 us; the launch traced here: 57.1 us
  Pallas kernels  53.4 us (93%)
  local copies, waits for them, and re-layouts  2.32 us (4%)
  other arithmetic  0.69 us (1%)
  between operations  0.69 us (1%)
    pallas_call x1, Pallas kernels, on_device(): pl.pallas_call(functools.partial(correlate_kernel, channels), out_shape=j...  26.8 us
    pallas_call x1, Pallas kernels, on_device(): pl.pallas_call(functools.partial(exchange_kernel, n), out_shape=(jax.Shap...  24.8 us
    unnamed x4, local copies, waits for them, and re-layouts  1.94 us
    pallas_call x1, Pallas kernels, on_device(): pl.pallas_call(functools.partial(prep_kernel, channels, groups), out_shap...  1.77 us

profile of v3, /device:TPU:1, one launch (start us, length us, event | category | flops | bytes accessed | tf_op | source)
XLA Modules:
  0.0 57.1 jit_solution(416262955419828555)
XLA Ops:
  0.7 0.7 %convert_element_type.3 = f32[1024]{0:T(1024)S(1)} convert(s32[1024]{0:T(1024)} %param.6) | non-fusion elementwise | flops 1024 | bytes 8192 | tf_op jit(solution)/shard_map/convert_element_type | solution.py:286
  1.3 0.1 dynamic-slice_bitcast_fusion
  1.4 0.1 dynamic_slice.6
  1.5 0.1 copy.8.ko_ref
  1.6 1.8 %shard_map.55 = (bf16[2,64,256]{2,1,0:T(8,128)(2,1)}, bf16[32,16,128]{2,1,0:T(8,128)(2,1)}) custom-call(s32[1]{0:T(128)} %copy.9.start_ref, bf16[64,1024]{1,0:T(8,128)(2,1)} %bitcast.10), custom_call_target="tpu_custom_call" | custom-call | tf_op jit(solution)/shard_map/pallas_call | solution.py:259
  3.4 0.1 copy.7.kb_ref
  3.5 24.8 %shard_map.56 = (bf16[2,32,64,256]{3,2,1,0:T(8,128)(2,1)}, bf16[32,16,128]{2,1,0:T(8,128)(2,1)}) custom-call(bf16[2,64,256]{2,1,0:T(8,128)(2,1)} %get-tuple-element.9.slab_ref, bf16[32,16,128]{2,1,0:T(8,128)(2,1)} %get-tuple-element.10.pack_ref), custom_call_target="tpu_custom_call" | custom-call | tf_op jit(solution)/shard_map/pallas_call | solution.py:268
  28.4 0.0 copy-start
  28.4 1.0 %copy-done = bf16[1024,256]{1,0:T(8,128)(2,1)S(1)} copy-done((bf16[1024,256]{1,0:T(8,128)(2,1)S(1)}, bf16[1024,256]{1,0:T(8,128)(2,1)}, u32[]{:S(2)}) %copy-start) | copy-done | bytes 524312
  29.4 0.0 copy-start.1
  29.4 0.9 %copy-done.1 = bf16[32,16,128]{2,1,0:T(8,128)(2,1)S(1)} copy-done((bf16[32,16,128]{2,1,0:T(8,128)(2,1)S(1)}, bf16[32,16,128]{2,1,0:T(8,128)(2,1)}, u32[]{:S(2)}) %copy-start.1) | copy-done | bytes 131096
  30.3 26.8 %shard_map.57 = bf16[512,32,256]{2,1,0:T(8,128)(2,1)} custom-call(bf16[2,2048,256]{2,1,0:T(8,128)(2,1)} %bitcast.9, bf16[32,16,128]{2,1,0:T(8,128)(2,1)S(1)} %copy-done.1, f32[512,1]{1,0:T(8,128)S(1)} %copy.7.kb_ref, f32[32,1]{1,0:T(8,128)S(1)} %copy.8.ko_ref, bf16[1024,1024]{1,0:T(8,128)(2,1)} %constant.14.clone.fwd_ref, bf16[1024,256]{1,0:T(8,128)(2,1)S(1)} %copy-done), custom_call_target="tpu_custom_call" | custom-call | tf_op jit(solution)/shard_map/pallas_call | solution.py:289
Async XLA Ops:
  28.4 1.0 %copy-start = (bf16[1024,256]{1,0:T(8,128)(2,1)S(1)}, bf16[1024,256]{1,0:T(8,128)(2,1)}, u32[]{:S(2)}) copy-start(bf16[1024,256]{1,0:T(8,128)(2,1)} %constant.15.clone.inv_ref) | copy-start | bytes 1572868
  29.4 0.9 %copy-start.1 = (bf16[32,16,128]{2,1,0:T(8,128)(2,1)S(1)}, bf16[32,16,128]{2,1,0:T(8,128)(2,1)}, u32[]{:S(2)}) copy-start(bf16[32,16,128]{2,1,0:T(8,128)(2,1)} %get-tuple-element.12.xo_ref) | copy-start | bytes 393220

commit v4 on v3

--- a/solution.py
+++ b/solution.py
@@ -13,7 +13,7 @@
 SEG = 2
 ROWS = 512
 F = 512
-SUB = 16
+SUB = 32
 
 
 def dft_tables():
@@ -152,6 +152,7 @@
         if pos == 0:
             for copy in local:
                 copy.start()
+        if pos == n // 8 - 1:
 
             @pl.loop(1, n)
             def _(d):

time: 57.4 us -> 57 us (level)
  no operation moved by 1% of the time
where the time goes in v4:
time: 57 us; the launch traced here: 56.7 us
  Pallas kernels  53.1 us (93%)
  local copies, waits for them, and re-layouts  2.32 us (4%)
  other arithmetic  0.69 us (1%)
  between operations  0.69 us (1%)
    pallas_call x1, Pallas kernels, on_device(): pl.pallas_call(functools.partial(correlate_kernel, channels), out_shape=j...  26.4 us
    pallas_call x1, Pallas kernels, on_device(): pl.pallas_call(functools.partial(exchange_kernel, n), out_shape=(jax.Shap...  24.9 us
    unnamed x4, local copies, waits for them, and re-layouts  1.94 us
    pallas_call x1, Pallas kernels, on_device(): pl.pallas_call(functools.partial(prep_kernel, channels, groups), out_shap...  1.77 us

profile of v4, /device:TPU:1, one launch (start us, length us, event | category | flops | bytes accessed | tf_op | source)
XLA Modules:
  0.0 56.7 jit_solution(15305900194881720489)
XLA Ops:
  0.7 0.7 %convert_element_type.3 = f32[1024]{0:T(1024)S(1)} convert(s32[1024]{0:T(1024)} %param.6) | non-fusion elementwise | flops 1024 | bytes 8192 | tf_op jit(solution)/shard_map/convert_element_type | solution.py:287
  1.3 0.1 dynamic-slice_bitcast_fusion
  1.4 0.1 dynamic_slice.6
  1.5 0.1 copy.8.ko_ref
  1.6 1.8 %shard_map.55 = (bf16[2,64,256]{2,1,0:T(8,128)(2,1)}, bf16[32,16,128]{2,1,0:T(8,128)(2,1)}) custom-call(s32[1]{0:T(128)} %copy.9.start_ref, bf16[64,1024]{1,0:T(8,128)(2,1)} %bitcast.10), custom_call_target="tpu_custom_call" | custom-call | tf_op jit(solution)/shard_map/pallas_call | solution.py:260
  3.4 0.1 copy.7.kb_ref
  3.5 24.9 %shard_map.56 = (bf16[2,32,64,256]{3,2,1,0:T(8,128)(2,1)}, bf16[32,16,128]{2,1,0:T(8,128)(2,1)}) custom-call(bf16[2,64,256]{2,1,0:T(8,128)(2,1)} %get-tuple-element.9.slab_ref, bf16[32,16,128]{2,1,0:T(8,128)(2,1)} %get-tuple-element.10.pack_ref), custom_call_target="tpu_custom_call" | custom-call | tf_op jit(solution)/shard_map/pallas_call | solution.py:269
  28.4 0.0 copy-start
  28.4 1.0 %copy-done = bf16[1024,256]{1,0:T(8,128)(2,1)S(1)} copy-done((bf16[1024,256]{1,0:T(8,128)(2,1)S(1)}, bf16[1024,256]{1,0:T(8,128)(2,1)}, u32[]{:S(2)}) %copy-start) | copy-done | bytes 524312
  29.4 0.0 copy-start.1
  29.4 0.9 %copy-done.1 = bf16[32,16,128]{2,1,0:T(8,128)(2,1)S(1)} copy-done((bf16[32,16,128]{2,1,0:T(8,128)(2,1)S(1)}, bf16[32,16,128]{2,1,0:T(8,128)(2,1)}, u32[]{:S(2)}) %copy-start.1) | copy-done | bytes 131096
  30.3 26.4 %shard_map.57 = bf16[512,32,256]{2,1,0:T(8,128)(2,1)} custom-call(bf16[2,2048,256]{2,1,0:T(8,128)(2,1)} %bitcast.9, bf16[32,16,128]{2,1,0:T(8,128)(2,1)S(1)} %copy-done.1, f32[512,1]{1,0:T(8,128)S(1)} %copy.7.kb_ref, f32[32,1]{1,0:T(8,128)S(1)} %copy.8.ko_ref, bf16[1024,1024]{1,0:T(8,128)(2,1)} %constant.14.clone.fwd_ref, bf16[1024,256]{1,0:T(8,128)(2,1)S(1)} %copy-done), custom_call_target="tpu_custom_call" | custom-call | tf_op jit(solution)/shard_map/pallas_call | solution.py:290
Async XLA Ops:
  28.4 1.0 %copy-start = (bf16[1024,256]{1,0:T(8,128)(2,1)S(1)}, bf16[1024,256]{1,0:T(8,128)(2,1)}, u32[]{:S(2)}) copy-start(bf16[1024,256]{1,0:T(8,128)(2,1)} %constant.15.clone.inv_ref) | copy-start | bytes 1572868
  29.4 0.9 %copy-start.1 = (bf16[32,16,128]{2,1,0:T(8,128)(2,1)S(1)}, bf16[32,16,128]{2,1,0:T(8,128)(2,1)}, u32[]{:S(2)}) copy-start(bf16[32,16,128]{2,1,0:T(8,128)(2,1)} %get-tuple-element.12.xo_ref) | copy-start | bytes 393220

commit v5 on v4

--- a/solution.py
+++ b/solution.py
@@ -175,9 +175,15 @@
 
 def correlate_kernel(
     channels, xb_ref, xo_ref, kb_ref, ko_ref, fwd_ref, inv_ref, out_ref,
-    wb, wo, cross_a, cross_b, out_buf, sems,
+    wb, wo, cross_a, cross_b, out_buf, sems, xb, xb_sems,
 ):
     groups = channels // 16
+
+    def copy_in(i):
+        return pltpu.make_async_copy(xb_ref.at[i], xb.at[i], xb_sems.at[i])
+
+    for i in range(2):
+        copy_in(i).start()
     dot0 = functools.partial(
         lax.dot_general, dimension_numbers=(((0,), (0,)), ((), ())),
         preferred_element_type=jnp.float32,
@@ -199,7 +205,8 @@
     @pl.loop(0, 2)
     def _(i):
         cols = pl.ds(pl.multiple_of(i * width, width), width)
-        band = [dot0(xb_ref[i, s * L:(s + 1) * L, :], fwd_ref[...]) for s in range(SEG)]
+        copy_in(i).wait()
+        band = [dot0(xb[i, s * L:(s + 1) * L, :], fwd_ref[...]) for s in range(SEG)]
         for q, part in enumerate(whiten(band[0], band[1], kb_ref[cols, :])):
             wb[cols, q * F:(q + 1) * F] = part.astype(jnp.float32)
 
@@ -290,7 +297,7 @@
     return pl.pallas_call(
         functools.partial(correlate_kernel, channels),
         out_shape=jax.ShapeDtypeStruct((ROWS, channels, LAGS), jnp.bfloat16),
-        in_specs=[vmem] * 6,
+        in_specs=[pl.BlockSpec(memory_space=pltpu.HBM)] + [vmem] * 5,
         out_specs=pl.BlockSpec(memory_space=pl.ANY),
         scratch_shapes=[
             pltpu.VMEM((ROWS, 4 * F), jnp.float32),
@@ -299,6 +306,8 @@
             pltpu.VMEM((SUB * channels, 2 * F), jnp.bfloat16),
             pltpu.VMEM((ROWS, channels, LAGS), jnp.bfloat16),
             pltpu.SemaphoreType.DMA((ROWS // (2 * SUB),)),
+            pltpu.VMEM((2, SEG * L, ROWS // 2), jnp.bfloat16),
+            pltpu.SemaphoreType.DMA((2,)),
         ],
         compiler_params=pltpu.CompilerParams(vmem_limit_bytes=52 * 2**20),
     )(band, own, keep_band, keep_own, jnp.asarray(forward), jnp.asarray(inverse))

time: 57 us -> 56.8 us (level)
  no operation moved by 1% of the time
where the time goes in v5:
time: 56.8 us; the launch traced here: 56.5 us
  Pallas kernels  52.8 us (93%)
  local copies, waits for them, and re-layouts  2.32 us (4%)
  other arithmetic  0.69 us (1%)
  between operations  0.69 us (1%)
    pallas_call x1, Pallas kernels, on_device(): pl.pallas_call(functools.partial(correlate_kernel, channels), out_shape=j...  26.2 us
    pallas_call x1, Pallas kernels, on_device(): pl.pallas_call(functools.partial(exchange_kernel, n), out_shape=(jax.Shap...  24.9 us
    unnamed x4, local copies, waits for them, and re-layouts  1.94 us
    pallas_call x1, Pallas kernels, on_device(): pl.pallas_call(functools.partial(prep_kernel, channels, groups), out_shap...  1.77 us

profile of v5, /device:TPU:1, one launch (start us, length us, event | category | flops | bytes accessed | tf_op | source)
XLA Modules:
  0.0 56.5 jit_solution(814043278274111083)
XLA Ops:
  0.7 0.7 %convert_element_type.3 = f32[1024]{0:T(1024)S(1)} convert(s32[1024]{0:T(1024)} %param.6) | non-fusion elementwise | flops 1024 | bytes 8192 | tf_op jit(solution)/shard_map/convert_element_type | solution.py:294
  1.3 0.1 dynamic-slice_bitcast_fusion
  1.4 0.1 dynamic_slice.6
  1.5 0.1 copy.8.ko_ref
  1.6 1.8 %shard_map.55 = (bf16[2,64,256]{2,1,0:T(8,128)(2,1)}, bf16[32,16,128]{2,1,0:T(8,128)(2,1)}) custom-call(s32[1]{0:T(128)} %copy.9.start_ref, bf16[64,1024]{1,0:T(8,128)(2,1)} %bitcast.10), custom_call_target="tpu_custom_call" | custom-call | tf_op jit(solution)/shard_map/pallas_call | solution.py:267
  3.4 0.1 copy.7.kb_ref
  3.5 24.9 %shard_map.56 = (bf16[2,32,64,256]{3,2,1,0:T(8,128)(2,1)}, bf16[32,16,128]{2,1,0:T(8,128)(2,1)}) custom-call(bf16[2,64,256]{2,1,0:T(8,128)(2,1)} %get-tuple-element.9.slab_ref, bf16[32,16,128]{2,1,0:T(8,128)(2,1)} %get-tuple-element.10.pack_ref), custom_call_target="tpu_custom_call" | custom-call | tf_op jit(solution)/shard_map/pallas_call | solution.py:276
  28.4 0.0 copy-start
  28.4 1.0 %copy-done = bf16[1024,256]{1,0:T(8,128)(2,1)S(1)} copy-done((bf16[1024,256]{1,0:T(8,128)(2,1)S(1)}, bf16[1024,256]{1,0:T(8,128)(2,1)}, u32[]{:S(2)}) %copy-start) | copy-done | bytes 524312
  29.4 0.0 copy-start.1
  29.4 0.9 %copy-done.1 = bf16[32,16,128]{2,1,0:T(8,128)(2,1)S(1)} copy-done((bf16[32,16,128]{2,1,0:T(8,128)(2,1)S(1)}, bf16[32,16,128]{2,1,0:T(8,128)(2,1)}, u32[]{:S(2)}) %copy-start.1) | copy-done | bytes 131096
  30.3 26.2 %shard_map.57 = bf16[512,32,256]{2,1,0:T(8,128)(2,1)} custom-call(bf16[2,2048,256]{2,1,0:T(8,128)(2,1)} %bitcast.9, bf16[32,16,128]{2,1,0:T(8,128)(2,1)S(1)} %copy-done.1, f32[512,1]{1,0:T(8,128)S(1)} %copy.7.kb_ref, f32[32,1]{1,0:T(8,128)S(1)} %copy.8.ko_ref, bf16[1024,1024]{1,0:T(8,128)(2,1)} %constant.14.clone.fwd_ref, bf16[1024,256]{1,0:T(8,128)(2,1)S(1)} %copy-done), custom_call_target="tpu_custom_call" | custom-call | tf_op jit(solution)/shard_map/pallas_call | solution.py:297
Async XLA Ops:
  28.4 1.0 %copy-start = (bf16[1024,256]{1,0:T(8,128)(2,1)S(1)}, bf16[1024,256]{1,0:T(8,128)(2,1)}, u32[]{:S(2)}) copy-start(bf16[1024,256]{1,0:T(8,128)(2,1)} %constant.15.clone.inv_ref) | copy-start | bytes 1572868
  29.4 0.9 %copy-start.1 = (bf16[32,16,128]{2,1,0:T(8,128)(2,1)S(1)}, bf16[32,16,128]{2,1,0:T(8,128)(2,1)}, u32[]{:S(2)}) copy-start(bf16[32,16,128]{2,1,0:T(8,128)(2,1)} %get-tuple-element.12.xo_ref) | copy-start | bytes 393220
